TPU v7x, 32 devices: a whole 2x2x4 slice. The times are simulated.
32 devices in a mesh: expert: 16 (over z, y, x), tensor: 2 (over core).
Axes of the slice: x: 2, y: 2, z: 4, core: 2. Of those that a mesh axis runs over, the one named last changes fastest.
Arguments:
- tokens: bfloat16 [2048, 7168], P('expert', 'tensor'), may hold values from -6 to 6
- out_grad: bfloat16 [2048, 7168], P('expert', 'tensor'), may hold values from -6 to 6
- gate_weight: bfloat16 [16, 7168, 2048], P('expert', None, 'tensor'), may hold values from -0.0625 to 0.0625
- up_weight: bfloat16 [16, 7168, 2048], P('expert', None, 'tensor'), may hold values from -0.0625 to 0.0625
- proj_hidden: bfloat16 [2048, 64], P('tensor'), may hold values from -0.125 to 0.125
- proj_grad: bfloat16 [7168, 64], P('tensor'), may hold values from -0.0625 to 0.0625
- expert_ids: int32 [2048, 8], P('expert'), may hold values from 0 to 15, all different within a row; in each aligned block of 128 rows (0 to 127, 128 to 255, ...) at most 96 rows name the same one
- weight_index: int32 [2048, 8], P('expert'), may hold values from 0 to 63
- weight_table: float32 [64], replicated, may hold values from 0.02 to 0.4
- sequence_ids: int32 [2048], P('expert'), may hold values from 0 to 3, never falling along the last dimension, each value on 1 to 1024 neighbouring positions
Outputs:
- features: float32 [16, 4, 4096], P('expert', None, 'tensor')
Inputs may be any that keep to these rules, and one draw needn't show every extreme that they name: `expert_ids`: within each aligned block of 128 tokens no expert is named by more than 96 tokens, a bound that some block reaches. `sequence_ids`: document ids never fall along the tokens; every document is present.
All inputs are finite; a program needn't handle non-finite values.
Results may differ from a plain program's by a relative error of at most 0.0029.
Values may be sent and summed in bfloat16 or wider, within the bound.
A program may use at most 192 MiB of HBM per device.

v0:
```python
import jax
import jax.numpy as jnp
from jax import lax
from jax.sharding import PartitionSpec as P

SEQS = 4


def slot_layout(expert_ids, weight_index, weight_table, sequence_ids, experts, capacity):
    tok_rows = expert_ids.shape[0]
    flat_ids = expert_ids.reshape(-1)
    picks = (flat_ids[:, None] == jnp.arange(experts, dtype=jnp.int32)[None, :]).astype(jnp.int32)
    running = jnp.cumsum(picks, axis=0) - 1
    slot_pos = jnp.sum(running * picks, axis=1)
    slot_index = flat_ids * capacity + slot_pos
    owners = jnp.arange(flat_ids.shape[0], dtype=jnp.int32) // expert_ids.shape[1]
    slot_token = jnp.full((experts * capacity,), tok_rows, jnp.int32).at[slot_index].set(owners)
    level_hits = (
        weight_index.reshape(-1)[:, None]
        == jnp.arange(weight_table.shape[0], dtype=jnp.int32)[None, :]
    )
    combine = jnp.sum(jnp.where(level_hits, weight_table[None, :], 0.0), axis=1)
    slot_weight = jnp.zeros((experts * capacity,), jnp.float32).at[slot_index].set(combine)
    slot_seq = (
        jnp.full((experts * capacity,), -1, jnp.int32).at[slot_index].set(sequence_ids[owners])
    )
    seq_weights = jnp.where(
        slot_seq[:, None] == jnp.arange(SEQS, dtype=jnp.int32)[None, :], slot_weight[:, None], 0.0
    )
    return (slot_token, seq_weights.reshape(experts, capacity, SEQS))


def pick_rows(source, slot_token, experts, capacity):
    padded = jnp.concatenate([source, jnp.zeros((1, source.shape[1]), source.dtype)], axis=0)
    return jnp.take(padded, slot_token, axis=0).reshape(experts, capacity, source.shape[1])


def local(
    tokens,
    out_grad,
    gate_weight,
    up_weight,
    proj_hidden,
    proj_grad,
    expert_ids,
    weight_index,
    weight_table,
    sequence_ids,
):
    experts = lax.axis_size("expert")
    tok_rows = tokens.shape[0]
    topk = expert_ids.shape[1]
    capacity = min(tok_rows, 3 * tok_rows * topk // (2 * experts))
    received = experts * capacity
    slot_token, seq_weights = slot_layout(
        expert_ids, weight_index, weight_table, sequence_ids, experts, capacity
    )
    feature_send = pick_rows(tokens, slot_token, experts, capacity)
    grad_send = pick_rows(out_grad, slot_token, experts, capacity)
    got_features, got_grads = (
        lax.all_to_all(feature_send, "expert", split_axis=0, concat_axis=0, tiled=True),
        lax.all_to_all(grad_send, "expert", split_axis=0, concat_axis=0, tiled=True),
    )
    got_weights = lax.all_to_all(seq_weights, "expert", split_axis=0, concat_axis=0, tiled=True)
    grad_part = jnp.dot(
        got_grads.reshape(received, -1), proj_grad, preferred_element_type=jnp.float32
    )
    projected = lax.psum(grad_part, "tensor")
    feature_block = got_features.reshape(received, -1)
    w_gate = gate_weight[0]
    w_up = up_weight[0]
    piece = lax.all_gather(feature_block, "tensor", axis=1, tiled=True)
    gate_sum = jnp.dot(piece, w_gate, preferred_element_type=jnp.float32)
    up_sum = jnp.dot(piece, w_up, preferred_element_type=jnp.float32)
    hidden = (jax.nn.silu(gate_sum) * up_sum).astype(jnp.bfloat16)
    left_part = jnp.dot(hidden, proj_hidden, preferred_element_type=jnp.float32)
    weights_flat = got_weights.reshape(received, SEQS)
    outer = jnp.einsum(
        "ts,tr,tq->srq", weights_flat, left_part, projected, precision=lax.Precision.HIGHEST
    )
    summed = lax.psum_scatter(outer.reshape(SEQS, -1), "tensor", scatter_dimension=1, tiled=True)
    return summed[None]


def solution(mesh):
    placed = (
        P("expert", "tensor"),
        P("expert", "tensor"),
        P("expert", None, "tensor"),
        P("expert", None, "tensor"),
        P("tensor", None),
        P("tensor", None),
        P("expert", None),
        P("expert", None),
        P(),
        P("expert"),
    )
    return jax.shard_map(
        local, mesh=mesh, in_specs=placed, out_specs=P("expert", None, "tensor"), check_vma=False
    )
```

profile of v0, /device:TPU:0, one launch (start us, length us, event | category | flops | bytes accessed | tf_op | source)
XLA Modules:
  0.0 683.6 jit_solution(9618285928207687477)
XLA Ops:
  6.5 0.8 copy.33
  7.6 0.7 broadcast_multiply_fusion
  8.3 4.5 reduce-window.6
  12.9 0.1 copy.35
  13.2 0.1 copy.32
  13.3 0.1 mul.28
  13.4 4.3 scatter_custom_fusion
  17.8 1.2 concatenate.6
  19.1 1.2 concatenate.7
  20.3 9.1 %gather_fusion.1 = bf16[1536,3584]{1,0:T(8,128)(2,1)} fusion(bf16[129,3584]{1,0:T(8,128)(2,1)S(1)} %concatenate.6, s32[2048]{0:T(1024)S(1)} %pad_clamp_fusion), kind=kCustom, calls=%fused_computation.clone | custom fusion | bytes 22026240 | tf_op jit(solution)/shard_map/jit(_take)/gather | solution.py:35
  29.4 9.1 %gather_fusion.2 = bf16[1536,3584]{1,0:T(8,128)(2,1)} fusion(bf16[129,3584]{1,0:T(8,128)(2,1)S(1)} %concatenate.7, s32[2048]{0:T(1024)S(1)} %pad_clamp_fusion), kind=kCustom, calls=%fused_computation.1.clone | custom fusion | bytes 22026240 | tf_op jit(solution)/shard_map/jit(_take)/gather | solution.py:35
  38.5 15.9 %broadcast_select_fusion = (bf16[1536,3584]{1,0:T(8,128)(2,1)}, bf16[1536,3584]{1,0:T(8,128)(2,1)}) fusion(bf16[1536,3584]{1,0:T(8,128)(2,1)} %gather_fusion.2, pred[1536]{0:T(1024)(128)(4,1)S(1)} %compare_and_fusion, bf16[1536,3584]{1,0:T(8,128)(2,1)} %gather_fusion.1), kind=kLoop, calls=%fused_computation.10 | loop fusion | flops 11010048 | bytes 44041728 | tf_op jit(solution)/shard_map/jit(_take)/select_n | solution.py:35
  54.4 8.5 %all-to-all-start = ((bf16[16,96,3584]{2,1,0:T(8,128)(2,1)}), bf16[16,96,3584]{2,1,0:T(8,128)(2,1)}, u32[]{:S(2)}, u32[]{:S(2)}) async-start(bf16[16,96,3584]{2,1,0:T(8,128)(2,1)} %bitcast.48), calls=%async_computation | async-start | bytes 22020096 | tf_op jit(solution)/shard_map/all_to_all | solution.py:61
  63.0 0.1 copy.37
  63.2 207.2 %all-to-all-done = bf16[16,96,3584]{2,1,0:T(8,128)(2,1)} async-done(((bf16[16,96,3584]{2,1,0:T(8,128)(2,1)}), bf16[16,96,3584]{2,1,0:T(8,128)(2,1)}, u32[]{:S(2)}, u32[]{:S(2)}) %all-to-all-start) | async-done | bytes 11010080 | tf_op jit(solution)/shard_map/all_to_all | solution.py:61
  270.4 0.1 select_reduce_fusion
  270.5 4.3 scatter_custom_fusion.2
  275.0 6.6 gather_fusion
  281.5 4.3 scatter_custom_fusion.1
  286.0 55.5 %all_to_all.15 = f32[16,96,4]{1,2,0:T(4,128)S(1)} all-to-all(f32[16,96,4]{1,2,0:T(4,128)S(1)} %fusion.17), channel_id=1, replica_groups=mesh['expert'=16,'tensor'=2] {'expert'}, dimensions={0} | all-to-all | bytes 49152 | tf_op jit(solution)/shard_map/all_to_all | solution.py:64
  341.5 4.9 all-to-all-start.2
  346.5 198.9 %all-to-all-done.2 = bf16[16,96,3584]{2,1,0:T(8,128)(2,1)} async-done(((bf16[16,96,3584]{2,1,0:T(8,128)(2,1)}), bf16[16,96,3584]{2,1,0:T(8,128)(2,1)}, u32[]{:S(2)}, u32[]{:S(2)}) %all-to-all-start.2) | async-done | bytes 11010080 | tf_op jit(solution)/shard_map/all_to_all | solution.py:62
  545.4 8.3 %fusion.28 = f32[1536,64]{0,1:T(8,128)} fusion(bf16[1536,3584]{1,0:T(8,128)(2,1)} %bitcast.10, bf16[3584,64]{0,1:T(8,128)(2,1)S(1)} %copy-done), kind=kOutput, calls=%fused_computation.55 | convolution fusion | flops 704643072 | bytes 11862016 | tf_op jit(solution)/shard_map/dot_general | solution.py:65
  553.7 0.2 reduce-scatter.4.cloned.1.call-start
  554.0 28.8 %fusion = f32[1536,1024]{1,0:T(8,128)S(1)} fusion(bf16[1536,7168]{1,0:T(8,128)(2,1)} %all-gather.2.cloned.1.call-done, bf16[1,7168,1024]{2,1,0:T(8,128)(2,1)} %param.15), kind=kOutput, calls=%fused_computation.6 | convolution fusion | flops 22548578304 | bytes 42991616 | tf_op jit(solution)/shard_map/dot_general | solution.py:74
  582.8 31.3 %multiply_convert_fusion = bf16[1536,1024]{1,0:T(8,128)(2,1)S(1)} fusion(f32[1536,1024]{1,0:T(8,128)S(1)} %fusion, bf16[1536,7168]{1,0:T(8,128)(2,1)} %all-gather.2.cloned.1.call-done, bf16[1,7168,1024]{2,1,0:T(8,128)(2,1)} %param.14), kind=kOutput, calls=%fused_computation.12 | convolution fusion | flops 22558015488 | bytes 46137344 | tf_op jit(solution)/shard_map/dot_general | solution.py:73
  614.1 1.1 fusion.27
  615.2 2.6 all-reduce.4.cloned.1.call-done
  617.8 2.4 fusion.8
  620.2 2.1 copy.41
  622.2 52.6 %reduce-scatter.4.cloned.1.call-done = f32[2048,4]{1,0:T(8,128)} async-done(((f32[4096,4]{1,0:T(8,128)}), f32[2048,4]{1,0:T(8,128)}) %reduce-scatter.4.cloned.1.call-update) | async-done | bytes 32784
  674.9 2.2 copy.40
  (40 shorter events, 1.1 us)
Async XLA Ops:
  6.5 538.9 %copy-start = (bf16[3584,64]{0,1:T(8,128)(2,1)S(1)}, bf16[3584,64]{0,1:T(8,128)(2,1)}, u32[]{:S(2)}) copy-start(bf16[3584,64]{0,1:T(8,128)(2,1)} %param.17) | copy-start | bytes 1376260
  54.4 8.6 %copy-start.4 = (s32[128,8]{0,1:T(8,128)S(1)}, s32[128,8]{0,1:T(8,128)}, u32[]{:S(2)}) copy-start(s32[128,8]{0,1:T(8,128)} %param.19) | copy-start | bytes 12292
  54.4 216.0 %all-to-all-start = ((bf16[16,96,3584]{2,1,0:T(8,128)(2,1)}), bf16[16,96,3584]{2,1,0:T(8,128)(2,1)}, u32[]{:S(2)}, u32[]{:S(2)}) async-start(bf16[16,96,3584]{2,1,0:T(8,128)(2,1)} %bitcast.48), calls=%async_computation | async-start | bytes 22020096 | tf_op jit(solution)/shard_map/all_to_all | solution.py:61
  62.9 207.5 %copy-start.5 = (f32[64]{0:T(128)S(1)}, f32[64]{0:T(128)}, u32[]{:S(2)}) copy-start(f32[64]{0:T(128)} %param.20) | copy-start | bytes 772
  62.9 212.0 %copy-start.2 = (s32[128]{0:T(128)S(1)}, s32[128]{0:T(128)}, u32[]{:S(2)}) copy-start(s32[128]{0:T(128)} %param.21) | copy-start | bytes 1540
  62.9 491.0 %all-gather.2.cloned.1.call-start = ((), (), s32[]{:S(2)}) async-start(), calls=%async_computation.4 | async-start | bytes 33030144 | tf_op jit(solution)/shard_map/all_gather | solution.py:72
  341.5 203.9 %all-to-all-start.2 = ((bf16[16,96,3584]{2,1,0:T(8,128)(2,1)}), bf16[16,96,3584]{2,1,0:T(8,128)(2,1)}, u32[]{:S(2)}, u32[]{:S(2)}) async-start(bf16[16,96,3584]{2,1,0:T(8,128)(2,1)} %bitcast.47), calls=%async_computation.2 | async-start | bytes 22020096 | tf_op jit(solution)/shard_map/all_to_all | solution.py:62
  346.4 271.4 %all-reduce.4.cloned.1.call-start = ((), (), s32[]{:S(2)}) async-start(), calls=%async_computation.5 | async-start | bytes 786432 | tf_op jit(solution)/shard_map/psum | solution.py:68
  553.7 121.2 %reduce-scatter.4.cloned.1.call-start = ((), (), s32[]{:S(2)}) async-start(), calls=%async_computation.6 | async-start | bytes 3145728
  582.8 31.3 %copy-start.3 = (bf16[1024,64]{0,1:T(8,128)(2,1)S(1)}, bf16[1024,64]{0,1:T(8,128)(2,1)}, u32[]{:S(2)}) copy-start(bf16[1024,64]{0,1:T(8,128)(2,1)} %param.16) | copy-start | bytes 393220
  582.8 94.2 %copy-start.1 = (bf16[3584,64]{0,1:T(8,128)(2,1)S(1)}, bf16[3584,64]{0,1:T(8,128)(2,1)}, u32[]{:S(2)}) copy-start(bf16[3584,64]{0,1:T(8,128)(2,1)} %param.17) | copy-start | bytes 1376260
Sparse Core Ops, SparseCore 0:
  270.5 79.5 all-gather.1
  553.8 63.8 all-reduce.3
  622.4 52.4 reduce-scatter.3
where the time goes:
time: 684 us
  waiting for transfers between devices  461 us (67%)
  matrix products  71.8 us (10%)
  blocking collectives  55.5 us (8%)
  local copies, waits for them, and re-layouts  46.4 us (7%)
  other arithmetic  21.5 us (3%)
  starting transfers between devices  13.7 us (2%)
  between operations  13.4 us (2%)
    all_to_all x1, waiting for transfers between devices, local(): lax.all_to_all(feature_send, 'expert', split_axis=0, concat_axis=0, tiled...  207 us
    all_to_all x1, waiting for transfers between devices, local(): lax.all_to_all(grad_send, 'expert', split_axis=0, concat_axis=0, tiled=True)  199 us
    all_to_all x1, blocking collectives, local(): lax.all_to_all(seq_weights, 'expert', split_axis=0, concat_axis=0, tiled=...  55.5 us
    unnamed x4, waiting for transfers between devices  52.7 us
    dot_general x1, matrix products, local(): gate_sum = jnp.dot(piece, w_gate, preferred_element_type=jnp.float32)  31.3 us
    dot_general x1, matrix products, local(): up_sum = jnp.dot(piece, w_up, preferred_element_type=jnp.float32)  28.8 us
    gather x2, local copies, waits for them, and re-layouts, pick_rows(): jnp.take(padded, slot_token, axis=0)  18.2 us
    select_n x2, other arithmetic, pick_rows(): jnp.take(padded, slot_token, axis=0)  15.9 us
  transfers between devices with their start and end apart: 5, of which 4 were waited for; matrix products, arithmetic and copies ran while one was open for 12% of the time, Pallas kernels for 0%

commit v1 on v0

v1 whole, which is shorter than its diff:
```python
import jax
import jax.numpy as jnp
from jax import lax
from jax.sharding import PartitionSpec as P

SEQS = 4


def small_rows(out_grad, proj_grad, expert_ids, weight_index, weight_table, sequence_ids):
    experts = lax.axis_size("expert")
    right = lax.psum(jnp.dot(out_grad, proj_grad, preferred_element_type=jnp.float32), "tensor")
    levels = jnp.arange(weight_table.shape[0], dtype=jnp.int32)
    combine = jnp.sum(
        jnp.where(weight_index[:, :, None] == levels, weight_table, 0.0), axis=2
    )
    hits = expert_ids[:, :, None] == jnp.arange(experts, dtype=jnp.int32)
    weights = jnp.sum(jnp.where(hits, combine[:, :, None], 0.0), axis=1)
    seq = sequence_ids.astype(jnp.float32)[:, None]
    packed = jnp.concatenate([right, weights, seq], axis=1)
    return lax.all_gather(packed, "expert", axis=0, tiled=True)


def combine_outer(left, packed, experts):
    width = packed.shape[1] - experts - 1
    right = packed[:, :width]
    weight = lax.dynamic_slice_in_dim(packed, width + lax.axis_index("expert"), 1, axis=1)
    seq = packed[:, width + experts :]
    by_seq = jnp.where(seq == jnp.arange(SEQS, dtype=jnp.float32)[None, :], weight, 0.0)
    scaled = (by_seq[:, :, None] * left[:, None, :]).reshape(left.shape[0], -1)
    outer = lax.dot_general(
        scaled, right, (((0,), (0,)), ((), ())), precision=lax.Precision.HIGHEST
    )
    summed = lax.psum_scatter(
        outer.reshape(SEQS, -1), "tensor", scatter_dimension=1, tiled=True
    )
    return summed[None]


def local(
    tokens,
    out_grad,
    gate_weight,
    up_weight,
    proj_hidden,
    proj_grad,
    expert_ids,
    weight_index,
    weight_table,
    sequence_ids,
):
    experts = lax.axis_size("expert")
    packed = small_rows(
        out_grad, proj_grad, expert_ids, weight_index, weight_table, sequence_ids
    )
    rows = lax.all_gather(tokens, "expert", axis=0, tiled=True)
    rows = lax.all_gather(rows, "tensor", axis=1, tiled=True)
    gate_sum = jnp.dot(rows, gate_weight[0], preferred_element_type=jnp.float32)
    up_sum = jnp.dot(rows, up_weight[0], preferred_element_type=jnp.float32)
    hidden = (jax.nn.silu(gate_sum) * up_sum).astype(jnp.bfloat16)
    left = jnp.dot(hidden, proj_hidden, preferred_element_type=jnp.float32)
    return combine_outer(left, packed, experts)


def solution(mesh):
    placed = (
        P("expert", "tensor"),
        P("expert", "tensor"),
        P("expert", None, "tensor"),
        P("expert", None, "tensor"),
        P("tensor", None),
        P("tensor", None),
        P("expert", None),
        P("expert", None),
        P(),
        P("expert"),
    )
    return jax.shard_map(
        local, mesh=mesh, in_specs=placed, out_specs=P("expert", None, "tensor"), check_vma=False
    )
```

time: 684 us -> 335 us (0.49)
  waiting for transfers between devices: 461 us -> 190 us
  local copies, waits for them, and re-layouts: 46.4 us -> 4.32 us
  other arithmetic: 21.5 us -> 0.38 us
  starting transfers between devices: 13.7 us -> 0.11 us
  blocking collectives: 55.5 us -> 45.3 us
  matrix products: 71.8 us -> 81.5 us
    all_to_all x2 -> x0, waiting for transfers between devices: 406 us -> none  [the longest x1 207 us: local(): lax.all_to_all(feature_send, 'expert', split_axis=0, concat_axis=0, tiled...]
    all_gather x1 -> x2, waiting for transfers between devices: 0.02 us -> 178 us  [the longest x1 177 us: local(): rows = lax.all_gather(tokens, 'expert', axis=0, tiled=True)]
    all_to_all x1 -> x0, blocking collectives: 55.5 us -> none  [local(): lax.all_to_all(seq_weights, 'expert', split_axis=0, concat_axis=0, tiled=...]
    all_gather x0 -> x1, blocking collectives: none -> 41.9 us  [small_rows(): return lax.all_gather(packed, 'expert', axis=0, tiled=True)]
    unnamed x4, waiting for transfers between devices: 52.7 us -> 11.6 us
    gather x3 -> x0, local copies, waits for them, and re-layouts: 24.7 us -> none  [the longest x2 18.2 us: pick_rows(): jnp.take(padded, slot_token, axis=0)]
    select_n x6 -> x1, other arithmetic: 16 us -> 0.01 us  [combine_outer(): jnp.where(seq == jnp.arange(SEQS, dtype=jnp.float32)[None, :], weight, 0.0)]
    all_to_all x2 -> x0, starting transfers between devices: 13.4 us -> none  [the longest x1 8.49 us: local(): lax.all_to_all(feature_send, 'expert', split_axis=0, concat_axis=0, tiled...]
  transfers between devices with their start and end apart: 5 -> 3, of which waited for: 4 -> 3; matrix products, arithmetic and copies ran while one was open for 12% -> 0% of each run, Pallas kernels for 0% -> 0%
where the time goes in v1:
time: 335 us; the launch traced here: 334 us
  waiting for transfers between devices  190 us (57%)
  matrix products  81.5 us (24%)
  blocking collectives  45.3 us (14%)
  between operations  13.3 us (4%)
  local copies, waits for them, and re-layouts  4.32 us (1%)
    all_gather x1, waiting for transfers between devices, local(): rows = lax.all_gather(tokens, 'expert', axis=0, tiled=True)  177 us
    all_gather x1, blocking collectives, small_rows(): return lax.all_gather(packed, 'expert', axis=0, tiled=True)  41.9 us
    dot_general x1, matrix products, local(): up_sum = jnp.dot(rows, up_weight[0], preferred_element_type=jnp.float32)  39.6 us
    dot_general x1, matrix products, local(): gate_sum = jnp.dot(rows, gate_weight[0], preferred_element_type=jnp.float32)  38.3 us
    unnamed x4, waiting for transfers between devices  11.6 us
  transfers between devices with their start and end apart: 3, of which 3 were waited for; matrix products, arithmetic and copies ran while one was open for 0% of the time, Pallas kernels for 0%

profile of v1, /device:TPU:0, one launch (start us, length us, event | category | flops | bytes accessed | tf_op | source)
XLA Modules:
  0.0 334.5 jit_solution(9104854321536373951)
XLA Ops:
  6.5 0.0 copy-start
  6.5 0.0 copy-start.2
  6.5 0.0 copy-start.7
  6.6 0.0 all-gather.3.cloned.1.call-start
  6.6 0.7 all-gather.3.cloned.1.call-update
  7.3 0.0 all-gather.5.cloned.1.call-start
  7.3 177.4 %all-gather.3.cloned.1.call-done = bf16[2048,3584]{1,0:T(8,128)(2,1)} async-done(((bf16[128,3584]{1,0:T(8,128)(2,1)}), bf16[2048,3584]{1,0:T(8,128)(2,1)}) %all-gather.3.cloned.1.call-update) | async-done | bytes 14680080 | tf_op jit(solution)/shard_map/all_gather | solution.py:55
  184.8 0.0 all-gather.5.cloned.1.call-update
  184.8 0.0 reduce-scatter.4.cloned.1.call-start
  184.8 0.0 copy-done
  184.9 0.0 copy-done.2
  184.9 0.4 fusion.10
  185.3 3.4 %psum.7 = f32[128,64]{0,1:T(8,128)S(1)} all-reduce(f32[128,64]{0,1:T(8,128)S(1)} %fusion.10), channel_id=1, replica_groups=mesh['expert'=16,'tensor'=2] {'tensor'}, use_global_device_ids=true, to_apply=%region_0.0 | all-reduce | flops 8192 | bytes 65536 | tf_op jit(solution)/shard_map/psum | solution.py:11
  188.7 0.0 copy-done.6
  188.7 0.0 copy-done.4
  188.7 0.1 select_reduce_fusion
  188.8 0.0 copy-done.5
  188.9 0.0 copy-done.7
  188.9 41.9 %all_gather.9 = f32[2048,81]{0,1:T(8,128)S(1)} all-gather(f32[128,81]{0,1:T(8,128)S(1)} %pad_maximum_fusion), channel_id=1, replica_groups=mesh['expert'=16,'tensor'=2] {'expert'}, dimensions={0}, use_global_device_ids=true | all-gather | bytes 705024 | tf_op jit(solution)/shard_map/all_gather | solution.py:20
  230.8 0.5 all-gather.5.cloned.1.call-done
  231.4 38.3 %fusion.2 = f32[2048,1024]{1,0:T(8,128)} fusion(bf16[2048,7168]{1,0:T(8,128)(2,1)} %all-gather.5.cloned.1.call-done, bf16[1,7168,1024]{2,1,0:T(8,128)(2,1)} %param.12), kind=kOutput, calls=%fused_computation.2 | convolution fusion | flops 30064771072 | bytes 52428800 | tf_op jit(solution)/shard_map/dot_general | solution.py:57
  269.7 39.6 %multiply_convert_fusion = bf16[2048,1024]{1,0:T(8,128)(2,1)S(1)} fusion(f32[2048,1024]{1,0:T(8,128)} %fusion.2, bf16[2048,7168]{1,0:T(8,128)(2,1)} %all-gather.5.cloned.1.call-done, bf16[1,7168,1024]{2,1,0:T(8,128)(2,1)} %param.13), kind=kOutput, calls=%fused_computation.4 | convolution fusion | flops 30077353984 | bytes 56623104 | tf_op jit(solution)/shard_map/dot_general | solution.py:58
  309.3 0.0 copy-done.3
  309.3 1.4 fusion.11
  310.7 0.2 broadcast_multiply_fusion
  310.9 1.8 fusion.6
  312.7 0.1 reshape.50
  312.8 2.0 copy.22
  314.8 0.0 reduce-scatter.4.cloned.1.call-update
  314.8 10.9 %reduce-scatter.4.cloned.1.call-done = f32[2048,4]{1,0:T(8,128)} async-done(((f32[4096,4]{1,0:T(8,128)}), f32[2048,4]{1,0:T(8,128)}) %reduce-scatter.4.cloned.1.call-update) | async-done | bytes 32784
  325.8 2.2 copy.23
  327.9 0.0 copy-done.1
  (10 shorter events, 0.1 us)
Async XLA Ops:
  6.5 178.3 %copy-start = (bf16[128,3584]{1,0:T(8,128)(2,1)S(1)}, bf16[128,3584]{1,0:T(8,128)(2,1)}, u32[]{:S(2)}) copy-start(bf16[128,3584]{1,0:T(8,128)(2,1)} %param.11) | copy-start | bytes 2752516
  6.5 178.3 %copy-start.2 = (bf16[3584,64]{0,1:T(8,128)(2,1)S(1)}, bf16[3584,64]{0,1:T(8,128)(2,1)}, u32[]{:S(2)}) copy-start(bf16[3584,64]{0,1:T(8,128)(2,1)} %param.15) | copy-start | bytes 1376260
  6.5 182.2 %copy-start.6 = (f32[64]{0:T(128)S(1)}, f32[64]{0:T(128)}, u32[]{:S(2)}) copy-start(f32[64]{0:T(128)} %param.18) | copy-start | bytes 772
  6.5 182.2 %copy-start.4 = (s32[128,8]{0,1:T(8,128)S(1)}, s32[128,8]{0,1:T(8,128)}, u32[]{:S(2)}) copy-start(s32[128,8]{0,1:T(8,128)} %param.17) | copy-start | bytes 12292
  6.5 182.3 %copy-start.5 = (s32[128,8]{0,1:T(8,128)S(1)}, s32[128,8]{0,1:T(8,128)}, u32[]{:S(2)}) copy-start(s32[128,8]{0,1:T(8,128)} %param.16) | copy-start | bytes 12292
  6.5 182.3 %copy-start.7 = (s32[128]{0:T(128)S(1)}, s32[128]{0:T(128)}, u32[]{:S(2)}) copy-start(s32[128]{0:T(128)} %param.19) | copy-start | bytes 1540
  6.6 178.2 %all-gather.3.cloned.1.call-start = ((), (), s32[]{:S(2)}) async-start(), calls=%async_computation.1 | async-start | bytes 15597568 | tf_op jit(solution)/shard_map/all_gather | solution.py:55
  7.3 224.1 %all-gather.5.cloned.1.call-start = ((), (), s32[]{:S(2)}) async-start(), calls=%async_computation.2 | async-start | bytes 44040192 | tf_op jit(solution)/shard_map/all_gather | solution.py:56
  184.8 141.0 %reduce-scatter.4.cloned.1.call-start = ((), (), s32[]{:S(2)}) async-start(), calls=%async_computation.3 | async-start | bytes 3145728
  269.7 39.6 %copy-start.3 = (bf16[1024,64]{0,1:T(8,128)(2,1)S(1)}, bf16[1024,64]{0,1:T(8,128)(2,1)}, u32[]{:S(2)}) copy-start(bf16[1024,64]{0,1:T(8,128)(2,1)} %param.14) | copy-start | bytes 393220
  269.7 58.2 %copy-start.1 = (bf16[128,3584]{1,0:T(8,128)(2,1)S(1)}, bf16[128,3584]{1,0:T(8,128)(2,1)}, u32[]{:S(2)}) copy-start(bf16[128,3584]{1,0:T(8,128)(2,1)} %param.11) | copy-start | bytes 2752516
Sparse Core Ops, SparseCore 0:
  10.2 174.5 all-gather.2
  186.3 44.9 all-gather.4
  315.0 10.7 reduce-scatter.3

commit v2 on v1

--- a/solution.py
+++ b/solution.py
@@ -1,9 +1,274 @@
 import jax
 import jax.numpy as jnp
 from jax import lax
+from jax.experimental import pallas as pl
+from jax.experimental.pallas import tpu as pltpu
 from jax.sharding import PartitionSpec as P
 
 SEQS = 4
+
+
+ORDER = (
+    "CX0 CY0 CO1 AO1 AX0 AY0 BO1 BY0 BX0 CO2 CD0 CX1 CY1 AX1 AY1 AD0 AO2 BX1 BO2 BD0 AX2 CO3 CD1 "
+    "BY1 CX2 CY2 AY2 BX2 AD1 BY2 AO3 AD2 BD1 BD2 BO3 AX3 AY3 CX3 CY3 CD2 BX3 BY3 AD3 BD3 CD3"
+).split()
+GROUP_ROWS = 256
+UNITS = 4
+MESH = pl.DeviceIdType.MESH
+
+
+def part_rows(rows):
+    big = rows * 3 // 8 // 16 * 16
+    return {"A": (0, big), "B": (big, big), "C": (2 * big, rows - 2 * big)}
+
+
+def make_groups(spans):
+    groups, now, held = [["AO0", "BO0", "CO0"]], [], 0
+    for name in ORDER:
+        size = spans[name[0]][1]
+        if held + size > GROUP_ROWS:
+            groups.append(now)
+            now, held = [], 0
+        now, held = now + [name], held + size
+    return groups + [now]
+
+
+def gather_kernel(
+    tok_ref,
+    wg_ref,
+    wu_ref,
+    ph_ref,
+    left_ref,
+    x,
+    wg,
+    wu,
+    acc,
+    recv_sem,
+    pair_sem,
+    send_sem,
+    own_sem,
+    weight_sem,
+):
+    rows, half = tok_ref.shape
+    spans = part_rows(rows)
+    groups = make_groups(spans)
+    cols = wg.shape[1] // UNITS
+    me, core = lax.axis_index("expert"), lax.axis_index("tensor")
+    mz, my, mx = me // 4, me // 2 % 2, me % 2
+    upper = mz // 2
+    inner = jnp.where(upper == 1, 3 - mz, mz)
+
+    def reflect(place):
+        return jnp.where(upper == 1, 3 - place, place)
+
+    def block_of(name):
+        step = int(name[2])
+        place = inner if step == 0 else 1 - inner if step == 1 else step
+        yy = 1 - my if name[1] in "YD" else my
+        xx = 1 - mx if name[1] in "XD" else mx
+        return (reflect(place) * 2 + yy) * 2 + xx
+
+    def device(link):
+        zz, yy, xx, cc = mz, my, mx, core
+        if link == "in":
+            zz = reflect(inner + 1)
+        elif link == "out":
+            zz = reflect(jnp.maximum(inner - 1, 0))
+        elif link == "x":
+            xx = 1 - mx
+        elif link == "y":
+            yy = 1 - my
+        else:
+            cc = 1 - core
+        return ((zz * 2 + yy) * 2 + xx, cc)
+
+    def piece(name, which):
+        start, size = spans[name[0]]
+        return x.at[which, block_of(name), pl.ds(start, size)]
+
+    def sem_index(name):
+        return "ABC".index(name[0]) * 16 + block_of(name)
+
+    sent = []
+
+    def send(name, link, when):
+        number = len(sent)
+        sems = pair_sem if link == "pair" else recv_sem
+
+        def build():
+            part = piece(name, core)
+            return pltpu.make_async_remote_copy(
+                src_ref=part,
+                dst_ref=part,
+                send_sem=send_sem.at[number],
+                recv_sem=sems.at[sem_index(name)],
+                device_id=device(link),
+                device_id_type=MESH,
+            )
+
+        if when is None:
+            build().start()
+        else:
+            pl.when(when)(lambda: build().start())
+        sent.append((build, when))
+
+    def sends(name):
+        part, column, step = name[0], name[1], int(name[2])
+        if column == "O" or part == "C":
+            if step == 0:
+                send(name, "in", None)
+                send(name, "out", inner == 1)
+            elif step == 1:
+                send(name, "in", inner == 1)
+            else:
+                send(name, "out", inner == 1)
+        if part == "C" and step > 0:
+            links = ""
+        elif column == "O":
+            links = "yx" if part == "B" else "xy"
+        elif column == "X":
+            links = "" if part == "B" else "y"
+        elif column == "Y":
+            links = "x" if part == "B" else ""
+        else:
+            links = ""
+        for link in links:
+            send(name, link, None)
+        send(name, "pair", None)
+
+    def landed(name, which, sems):
+        part = piece(name, which)
+        pltpu.make_async_remote_copy(
+            src_ref=part,
+            dst_ref=part,
+            send_sem=send_sem.at[0],
+            recv_sem=sems.at[sem_index(name)],
+            device_id=device("pair"),
+            device_id_type=MESH,
+        ).wait_recv()
+
+    own = pltpu.make_async_copy(tok_ref, x.at[core, me], own_sem)
+    own.start()
+    loads = []
+    for n in range(UNITS):
+        for at, (src, dst) in enumerate(((wg_ref, wg), (wu_ref, wu))):
+            load = pltpu.make_async_copy(
+                src.at[0, :, pl.ds(n * cols, cols)],
+                dst.at[:, pl.ds(n * cols, cols)],
+                weight_sem.at[2 * n + at],
+            )
+            loads.append(load)
+
+    barrier = pltpu.get_barrier_semaphore()
+    for link in ("in", "x", "y", "pair"):
+        pl.semaphore_signal(barrier, inc=1, device_id=device(link), device_id_type=MESH)
+
+    @pl.when(inner == 1)
+    def _():
+        pl.semaphore_signal(barrier, inc=1, device_id=device("out"), device_id_type=MESH)
+
+    pl.semaphore_wait(barrier, 4 + inner)
+    own.wait()
+    for name in ("CO0", "AO0", "BO0"):
+        sends(name)
+    for load in loads:
+        load.start()
+
+    def unit(group, n):
+        size = sum(spans[name[0]][1] for name in group)
+        if n == 0:
+            for name in group:
+                landed(name, 1 - core, pair_sem)
+        if group[0] == "AO0":
+            loads[2 * n].wait()
+            loads[2 * n + 1].wait()
+        blocks = [(block_of(name),) + spans[name[0]] for name in group]
+        wide = pl.ds(n * cols, cols)
+
+        def step(i, carry):
+            lanes = pl.ds(pl.multiple_of(i % 2 * (half // 2), 128), half // 2)
+            deep = pl.ds(pl.multiple_of(i * (half // 2), 128), half // 2)
+            lhs = jnp.concatenate(
+                [x[i // 2, at, pl.ds(start, count), lanes] for at, start, count in blocks], axis=0
+            )
+            gate = jnp.dot(lhs, wg[deep, wide], preferred_element_type=jnp.float32)
+            up = jnp.dot(lhs, wu[deep, wide], preferred_element_type=jnp.float32)
+            acc[0, pl.ds(0, size)] = jnp.where(i > 0, acc[0, pl.ds(0, size)], 0.0) + gate
+            acc[1, pl.ds(0, size)] = jnp.where(i > 0, acc[1, pl.ds(0, size)], 0.0) + up
+            return carry
+
+        lax.fori_loop(0, 4, step, 0)
+        gate, up = acc[0, pl.ds(0, size)], acc[1, pl.ds(0, size)]
+        hidden = (gate / (1.0 + jnp.exp(-gate)) * up).astype(jnp.bfloat16)
+        part = jnp.dot(hidden, ph_ref[wide], preferred_element_type=jnp.float32)
+        done = 0
+        for at, start, count in blocks:
+            piece_rows = part[done : done + count]
+            if n > 0:
+                piece_rows = piece_rows + left_ref[at, pl.ds(start, count)]
+            left_ref[at, pl.ds(start, count)] = piece_rows
+            done += count
+
+    for g in range(1, len(groups) + 1):
+        waiting = list(groups[g]) if g < len(groups) else []
+        per = -(-len(waiting) // UNITS)
+        for n in range(UNITS):
+            unit(groups[g - 1], n)
+            for name in waiting[n * per : (n + 1) * per]:
+                landed(name, core, recv_sem)
+                sends(name)
+
+    for build, when in sent:
+        if when is None:
+            build().wait_send()
+        else:
+            pl.when(when)(lambda build=build: build().wait_send())
+
+
+def count_sends():
+    total = 0
+    for name in ["AO0", "BO0", "CO0"] + ORDER:
+        part, column, step = name[0], name[1], int(name[2])
+        if column == "O" or part == "C":
+            total += 2 if step == 0 else 1
+        if not (part == "C" and step > 0):
+            total += {"O": 2, "X": int(part != "B"), "Y": int(part == "B"), "D": 0}[column]
+        total += 1
+    return total
+
+
+def gathered_left(tokens, gate_weight, up_weight, proj_hidden):
+    experts = lax.axis_size("expert")
+    rows, half = tokens.shape
+    _, deep, wide = gate_weight.shape
+    width = proj_hidden.shape[1]
+    left = pl.pallas_call(
+        gather_kernel,
+        out_shape=jax.ShapeDtypeStruct((experts, rows, width), jnp.float32),
+        in_specs=[pl.BlockSpec(memory_space=pl.ANY)] * 3
+        + [pl.BlockSpec(memory_space=pltpu.VMEM)],
+        out_specs=pl.BlockSpec(memory_space=pltpu.VMEM),
+        scratch_shapes=[
+            pltpu.VMEM((2, experts, rows, half), jnp.bfloat16),
+            pltpu.VMEM((deep, wide), jnp.bfloat16),
+            pltpu.VMEM((deep, wide), jnp.bfloat16),
+            pltpu.VMEM((2, GROUP_ROWS, wide // UNITS), jnp.float32),
+            pltpu.SemaphoreType.DMA((3 * experts,)),
+            pltpu.SemaphoreType.DMA((3 * experts,)),
+            pltpu.SemaphoreType.DMA((count_sends(),)),
+            pltpu.SemaphoreType.DMA,
+            pltpu.SemaphoreType.DMA((2 * UNITS,)),
+        ],
+        compiler_params=pltpu.CompilerParams(
+            collective_id=0, has_side_effects=True, vmem_limit_bytes=62 * 2**20
+        ),
+        cost_estimate=pl.CostEstimate(
+            flops=4 * experts * rows * deep * wide,
+            bytes_accessed=4 * deep * wide + 2 * rows * half,
+            transcendentals=experts * rows * wide,
+        ),
+    )(tokens, gate_weight, up_weight, proj_hidden)
+    return left.reshape(experts * rows, width)
 
 
 def small_rows(out_grad, proj_grad, expert_ids, weight_index, weight_table, sequence_ids):
@@ -52,6 +317,9 @@
     packed = small_rows(
         out_grad, proj_grad, expert_ids, weight_index, weight_table, sequence_ids
     )
+    if experts == 16 and lax.axis_size("tensor") == 2:
+        left = gathered_left(tokens, gate_weight, up_weight, proj_hidden)
+        return combine_outer(left, packed, experts)
     rows = lax.all_gather(tokens, "expert", axis=0, tiled=True)
     rows = lax.all_gather(rows, "tensor", axis=1, tiled=True)
     gate_sum = jnp.dot(rows, gate_weight[0], preferred_element_type=jnp.float32)

time: 335 us -> 230 us (0.69)
  waiting for transfers between devices: 190 us -> 11.5 us
  Pallas kernels: 0 us -> 141 us
  matrix products: 81.5 us -> 3.21 us
  blocking collectives: 45.3 us -> 50.3 us
  local copies, waits for them, and re-layouts: 4.32 us -> 8.05 us
    all_gather x2 -> x0, waiting for transfers between devices: 178 us -> none  [the longest x1 177 us: local(): rows = lax.all_gather(tokens, 'expert', axis=0, tiled=True)]
    pallas_call x0 -> x1, Pallas kernels: none -> 141 us  [gathered_left(): pl.pallas_call(gather_kernel, out_shape=jax.ShapeDtypeStruct((experts, ro...]
    dot_general x3 -> x0, matrix products: 79.3 us -> none  [the longest x1 39.6 us: local(): up_sum = jnp.dot(rows, up_weight[0], preferred_element_type=jnp.float32)]
    all_gather x1, blocking collectives: 41.9 us -> 46.6 us  [small_rows(): return lax.all_gather(packed, 'expert', axis=0, tiled=True)]
    unnamed x4 -> x2, waiting for transfers between devices: 11.6 us -> 11.5 us
  transfers between devices with their start and end apart: 3 -> 1, of which waited for: 3 -> 1; matrix products, arithmetic and copies ran while one was open for 0% -> 0% of each run, Pallas kernels for 0% -> 0%
where the time goes in v2:
time: 230 us
  Pallas kernels  141 us (61%)
  blocking collectives  50.3 us (22%)
  between operations  13.5 us (6%)
  waiting for transfers between devices  11.5 us (5%)
  local copies, waits for them, and re-layouts  8.05 us (4%)
  matrix products  3.21 us (1%)
  other arithmetic  2.5 us (1%)
    pallas_call x1, Pallas kernels, gathered_left(): pl.pallas_call(gather_kernel, out_shape=jax.ShapeDtypeStruct((experts, ro...  141 us
    all_gather x1, blocking collectives, small_rows(): return lax.all_gather(packed, 'expert', axis=0, tiled=True)  46.6 us
    unnamed x2, waiting for transfers between devices  11.5 us
    unnamed x5, local copies, waits for them, and re-layouts  6.38 us
  transfers between devices with their start and end apart: 1, of which 1 were waited for; matrix products, arithmetic and copies ran while one was open for 0% of the time, Pallas kernels for 0%

profile of v2, /device:TPU:0, one launch (start us, length us, event | category | flops | bytes accessed | tf_op | source)
XLA Modules:
  0.0 229.6 jit_solution(18263966262728022894)
XLA Ops:
  6.5 0.0 copy-start
  6.5 0.0 reduce-scatter.4.cloned.1.call-start
  6.5 0.7 convert_bitcast_fusion
  7.3 0.5 copy-done
  7.7 1.4 fusion.4
  9.2 3.7 %psum.7 = f32[128,64]{0,1:T(8,128)S(1)} all-reduce(f32[128,64]{0,1:T(8,128)S(1)} %fusion.4), channel_id=1, replica_groups=mesh['expert'=16,'tensor'=2] {'tensor'}, use_global_device_ids=true, to_apply=%region_0.0 | all-reduce | flops 8192 | bytes 65536 | tf_op jit(solution)/shard_map/psum | solution.py:276
  12.9 1.8 copy.24.ph_ref
  14.6 0.8 select_reduce_fusion
  15.4 0.7 select_reduce_fusion.1
  16.2 46.6 %all_gather.3 = f32[2048,81]{0,1:T(8,128)S(1)} all-gather(f32[128,81]{0,1:T(8,128)S(1)} %pad_maximum_fusion), channel_id=1, replica_groups=mesh['expert'=16,'tensor'=2] {'expert'}, dimensions={0}, use_global_device_ids=true | all-gather | bytes 705024 | tf_op jit(solution)/shard_map/all_gather | solution.py:285
  62.8 140.5 %shard_map.100 = f32[16,128,64]{2,1,0:T(8,128)} custom-call(bf16[128,3584]{1,0:T(8,128)(2,1)} %tok_ref.1, bf16[1,7168,1024]{2,1,0:T(8,128)(2,1)} %wg_ref.1, bf16[1,7168,1024]{2,1,0:T(8,128)(2,1)} %wu_ref.1, bf16[1024,64]{1,0:T(8,128)(2,1)} %copy.24.ph_ref), custom_call_target="tpu_custom_call" | custom-call | flops 60129542144 | bytes 30277632 | tf_op jit(solution)/shard_map/pallas_call | solution.py:245
  203.3 1.5 copy.25
  204.9 0.2 broadcast_multiply_fusion
  205.1 1.8 fusion
  206.9 0.1 reshape.50
  207.0 2.0 copy.28
  209.0 0.0 reduce-scatter.4.cloned.1.call-update
  209.1 11.5 %reduce-scatter.4.cloned.1.call-done = f32[2048,4]{1,0:T(8,128)} async-done(((f32[4096,4]{1,0:T(8,128)}), f32[2048,4]{1,0:T(8,128)}) %reduce-scatter.4.cloned.1.call-update) | async-done | bytes 32784
  220.6 2.2 copy.29
  (3 shorter events, 0.0 us)
Async XLA Ops:
  6.5 1.2 copy-start
  6.5 214.0 %reduce-scatter.4.cloned.1.call-start = ((), (), s32[]{:S(2)}) async-start(), calls=%async_computation.1 | async-start | bytes 3145728
Sparse Core Ops, SparseCore 0:
  209.2 11.3 reduce-scatter.3

commit v3 on v2

--- a/solution.py
+++ b/solution.py
@@ -9,10 +9,13 @@
 
 
 ORDER = (
-    "CX0 CY0 CO1 AO1 AX0 AY0 BO1 BY0 BX0 CO2 CD0 CX1 CY1 AX1 AY1 AD0 AO2 BX1 BO2 BD0 AX2 CO3 CD1 "
-    "BY1 CX2 CY2 AY2 BX2 AD1 BY2 AO3 AD2 BD1 BD2 BO3 AX3 AY3 CX3 CY3 CD2 BX3 BY3 AD3 BD3 CD3"
-).split()
-GROUP_ROWS = 256
+    "CX0", "CY0", "CO1", "AO1", "AX0", "AY0", "BO1", "SO1", "BY0", "SY0", "BX0", "SX0", "CO2",
+    "CD0", "CX1", "CY1", "AX1", "AY1", "AD0", "AO2", "BX1", "SX1", "BO2", "SO2", "BD0", "SD0",
+    "AX2", "CO3", "CD1", "BY1", "SY1", "CX2", "CY2", "AY2", "BX2", "SX2", "AD1", "BY2", "SY2",
+    "AO3", "AD2", "BD1", "SD1", "BD2", "SD2", "BO3", "SO3", "AX3", "AY3", "CX3", "CY3", "CD2",
+    "BX3", "SX3", "BY3", "SY3", "AD3", "BD3", "SD3", "CD3",
+)
+GROUP_ROWS = (256, 512, 512, 384, 256)
 UNITS = 4
 MESH = pl.DeviceIdType.MESH
 
@@ -23,14 +26,21 @@
 
 
 def make_groups(spans):
-    groups, now, held = [["AO0", "BO0", "CO0"]], [], 0
+    groups, sizes, now, held = [["AO0", "BO0", "CO0"]], list(GROUP_ROWS), [], 0
     for name in ORDER:
-        size = spans[name[0]][1]
-        if held + size > GROUP_ROWS:
+        size = spans[name[0]][1] if name[0] != "S" else 0
+        if held + size > sizes[0] and len(sizes) > 1:
             groups.append(now)
             now, held = [], 0
+            sizes.pop(0)
         now, held = now + [name], held + size
     return groups + [now]
+
+
+def most_rows(spans):
+    return max(
+        sum(spans[name[0]][1] for name in group if name[0] != "S") for group in make_groups(spans)
+    )
 
 
 def gather_kernel(
@@ -38,16 +48,23 @@
     wg_ref,
     wu_ref,
     ph_ref,
+    small_ref,
+    out_ref,
     left_ref,
     x,
     wg,
     wu,
     acc,
+    small,
+    partner,
+    full,
+    other,
     recv_sem,
     pair_sem,
     send_sem,
     own_sem,
     weight_sem,
+    swap_sem,
 ):
     rows, half = tok_ref.shape
     spans = part_rows(rows)
@@ -83,11 +100,13 @@
         return ((zz * 2 + yy) * 2 + xx, cc)
 
     def piece(name, which):
+        if name[0] == "S":
+            return small.at[block_of(name), pl.ds(which * (rows // 2), rows // 2)]
         start, size = spans[name[0]]
         return x.at[which, block_of(name), pl.ds(start, size)]
 
     def sem_index(name):
-        return "ABC".index(name[0]) * 16 + block_of(name)
+        return "ABCS".index(name[0]) * 16 + block_of(name)
 
     sent = []
 
@@ -125,11 +144,11 @@
         if part == "C" and step > 0:
             links = ""
         elif column == "O":
-            links = "yx" if part == "B" else "xy"
+            links = "yx" if part in "BS" else "xy"
         elif column == "X":
-            links = "" if part == "B" else "y"
+            links = "" if part in "BS" else "y"
         elif column == "Y":
-            links = "x" if part == "B" else ""
+            links = "x" if part in "BS" else ""
         else:
             links = ""
         for link in links:
@@ -168,13 +187,33 @@
         pl.semaphore_signal(barrier, inc=1, device_id=device("out"), device_id_type=MESH)
 
     pl.semaphore_wait(barrier, 4 + inner)
+
+    def swap(src, dst, number):
+        return pltpu.make_async_remote_copy(
+            src_ref=src,
+            dst_ref=dst,
+            send_sem=swap_sem.at[2 * number],
+            recv_sem=swap_sem.at[2 * number + 1],
+            device_id=device("pair"),
+            device_id_type=MESH,
+        )
+
+    share = rows // 2
+    mine = pl.ds(pl.multiple_of(core * share, share), share)
+    theirs = pl.ds(pl.multiple_of((1 - core) * share, share), share)
+    partial = swap(small_ref.at[theirs], partner, 0)
+    partial.start()
     own.wait()
     for name in ("CO0", "AO0", "BO0"):
         sends(name)
+    partial.wait()
+    small[me, mine] = small_ref[mine] + partner[...]
+    sends("SO0")
     for load in loads:
         load.start()
 
-    def unit(group, n):
+    def unit(group, n, handle):
+        group = [name for name in group if name[0] != "S"]
         size = sum(spans[name[0]][1] for name in group)
         if n == 0:
             for name in group:
@@ -197,7 +236,9 @@
             acc[1, pl.ds(0, size)] = jnp.where(i > 0, acc[1, pl.ds(0, size)], 0.0) + up
             return carry
 
-        lax.fori_loop(0, 4, step, 0)
+        lax.fori_loop(0, 2, step, 0)
+        handle()
+        lax.fori_loop(2, 4, step, 0)
         gate, up = acc[0, pl.ds(0, size)], acc[1, pl.ds(0, size)]
         hidden = (gate / (1.0 + jnp.exp(-gate)) * up).astype(jnp.bfloat16)
         part = jnp.dot(hidden, ph_ref[wide], preferred_element_type=jnp.float32)
@@ -208,15 +249,55 @@
                 piece_rows = piece_rows + left_ref[at, pl.ds(start, count)]
             left_ref[at, pl.ds(start, count)] = piece_rows
             done += count
+        handle()
 
     for g in range(1, len(groups) + 1):
         waiting = list(groups[g]) if g < len(groups) else []
-        per = -(-len(waiting) // UNITS)
-        for n in range(UNITS):
-            unit(groups[g - 1], n)
-            for name in waiting[n * per : (n + 1) * per]:
+        per = -(-len(waiting) // (2 * UNITS))
+
+        def handle():
+            for name in waiting[:per]:
                 landed(name, core, recv_sem)
                 sends(name)
+            del waiting[:per]
+
+        for n in range(UNITS):
+            unit(groups[g - 1], n, handle)
+
+    for name in ("SO0",) + ORDER:
+        if name[0] == "S":
+            landed(name, 1 - core, pair_sem)
+    width = left_ref.shape[2]
+    experts = x.shape[1]
+    together = 4
+
+    def outer(i, carry):
+        held = pl.ds(i * together, together)
+        packed = small[held].reshape(together * rows, small.shape[2])
+        left = left_ref[held].reshape(together * rows, width)
+        lane = lax.broadcasted_iota(jnp.int32, packed.shape, 1)
+        weight = jnp.sum(jnp.where(lane == width + me, packed, 0.0), axis=1, keepdims=True)
+        seq = packed[:, width + experts : width + experts + 1]
+        for s in range(SEQS):
+            scaled = left * jnp.where(seq == float(s), weight, 0.0)
+            term = lax.dot_general(
+                scaled,
+                packed,
+                (((0,), (0,)), ((), ())),
+                precision=lax.Precision.HIGHEST,
+                preferred_element_type=jnp.float32,
+            )
+            full[s] = jnp.where(i > 0, full[s], 0.0) + term
+        return carry
+
+    lax.fori_loop(0, experts // together, outer, 0)
+    share = width // 2
+    mine = pl.ds(pl.multiple_of(core * share, share), share)
+    theirs = pl.ds(pl.multiple_of((1 - core) * share, share), share)
+    last = swap(full.at[:, theirs], other, 1)
+    last.start()
+    last.wait()
+    out_ref[...] = (full[:, mine] + other[...])[:, :, :width]
 
     for build, when in sent:
         if when is None:
@@ -227,37 +308,45 @@
 
 def count_sends():
     total = 0
-    for name in ["AO0", "BO0", "CO0"] + ORDER:
+    for name in ("AO0", "BO0", "CO0", "SO0") + ORDER:
         part, column, step = name[0], name[1], int(name[2])
         if column == "O" or part == "C":
             total += 2 if step == 0 else 1
         if not (part == "C" and step > 0):
-            total += {"O": 2, "X": int(part != "B"), "Y": int(part == "B"), "D": 0}[column]
+            total += {"O": 2, "X": int(part not in "BS"), "Y": int(part in "BS"), "D": 0}[column]
         total += 1
     return total
 
 
-def gathered_left(tokens, gate_weight, up_weight, proj_hidden):
+def gathered_features(tokens, gate_weight, up_weight, proj_hidden, small):
     experts = lax.axis_size("expert")
     rows, half = tokens.shape
     _, deep, wide = gate_weight.shape
     width = proj_hidden.shape[1]
-    left = pl.pallas_call(
+    lanes = small.shape[1]
+    f32, bf16 = jnp.float32, jnp.bfloat16
+    return pl.pallas_call(
         gather_kernel,
-        out_shape=jax.ShapeDtypeStruct((experts, rows, width), jnp.float32),
+        out_shape=jax.ShapeDtypeStruct((SEQS, width // 2, width), f32),
         in_specs=[pl.BlockSpec(memory_space=pl.ANY)] * 3
-        + [pl.BlockSpec(memory_space=pltpu.VMEM)],
+        + [pl.BlockSpec(memory_space=pltpu.VMEM)] * 2,
         out_specs=pl.BlockSpec(memory_space=pltpu.VMEM),
         scratch_shapes=[
-            pltpu.VMEM((2, experts, rows, half), jnp.bfloat16),
-            pltpu.VMEM((deep, wide), jnp.bfloat16),
-            pltpu.VMEM((deep, wide), jnp.bfloat16),
-            pltpu.VMEM((2, GROUP_ROWS, wide // UNITS), jnp.float32),
-            pltpu.SemaphoreType.DMA((3 * experts,)),
-            pltpu.SemaphoreType.DMA((3 * experts,)),
+            pltpu.VMEM((experts, rows, width), f32),
+            pltpu.VMEM((2, experts, rows, half), bf16),
+            pltpu.VMEM((deep, wide), bf16),
+            pltpu.VMEM((deep, wide), bf16),
+            pltpu.VMEM((2, most_rows(part_rows(rows)), wide // UNITS), f32),
+            pltpu.VMEM((experts, rows, lanes), f32),
+            pltpu.VMEM((rows // 2, lanes), f32),
+            pltpu.VMEM((SEQS, width, lanes), f32),
+            pltpu.VMEM((SEQS, width // 2, lanes), f32),
+            pltpu.SemaphoreType.DMA((4 * experts,)),
+            pltpu.SemaphoreType.DMA((4 * experts,)),
             pltpu.SemaphoreType.DMA((count_sends(),)),
             pltpu.SemaphoreType.DMA,
             pltpu.SemaphoreType.DMA((2 * UNITS,)),
+            pltpu.SemaphoreType.DMA((4,)),
         ],
         compiler_params=pltpu.CompilerParams(
             collective_id=0, has_side_effects=True, vmem_limit_bytes=62 * 2**20
@@ -267,22 +356,18 @@
             bytes_accessed=4 * deep * wide + 2 * rows * half,
             transcendentals=experts * rows * wide,
         ),
-    )(tokens, gate_weight, up_weight, proj_hidden)
-    return left.reshape(experts * rows, width)
-
-
-def small_rows(out_grad, proj_grad, expert_ids, weight_index, weight_table, sequence_ids):
+    )(tokens, gate_weight, up_weight, proj_hidden, small)
+
+
+def small_rows(expert_ids, weight_index, weight_table, sequence_ids):
     experts = lax.axis_size("expert")
-    right = lax.psum(jnp.dot(out_grad, proj_grad, preferred_element_type=jnp.float32), "tensor")
     levels = jnp.arange(weight_table.shape[0], dtype=jnp.int32)
     combine = jnp.sum(
         jnp.where(weight_index[:, :, None] == levels, weight_table, 0.0), axis=2
     )
     hits = expert_ids[:, :, None] == jnp.arange(experts, dtype=jnp.int32)
     weights = jnp.sum(jnp.where(hits, combine[:, :, None], 0.0), axis=1)
-    seq = sequence_ids.astype(jnp.float32)[:, None]
-    packed = jnp.concatenate([right, weights, seq], axis=1)
-    return lax.all_gather(packed, "expert", axis=0, tiled=True)
+    return jnp.concatenate([weights, sequence_ids.astype(jnp.float32)[:, None]], axis=1)
 
 
 def combine_outer(left, packed, experts):
@@ -314,12 +399,16 @@
     sequence_ids,
 ):
     experts = lax.axis_size("expert")
-    packed = small_rows(
-        out_grad, proj_grad, expert_ids, weight_index, weight_table, sequence_ids
-    )
+    small = small_rows(expert_ids, weight_index, weight_table, sequence_ids)
+    right = jnp.dot(out_grad, proj_grad, preferred_element_type=jnp.float32)
     if experts == 16 and lax.axis_size("tensor") == 2:
-        left = gathered_left(tokens, gate_weight, up_weight, proj_hidden)
-        return combine_outer(left, packed, experts)
+        small = jnp.where(lax.axis_index("tensor") == 0, small, 0.0)
+        packed = jnp.concatenate([right, small], axis=1)
+        packed = jnp.pad(packed, ((0, 0), (0, -packed.shape[1] % 128)))
+        features = gathered_features(tokens, gate_weight, up_weight, proj_hidden, packed)
+        return features.reshape(1, SEQS, -1)
+    packed = jnp.concatenate([lax.psum(right, "tensor"), small], axis=1)
+    packed = lax.all_gather(packed, "expert", axis=0, tiled=True)
     rows = lax.all_gather(tokens, "expert", axis=0, tiled=True)
     rows = lax.all_gather(rows, "tensor", axis=1, tiled=True)
     gate_sum = jnp.dot(rows, gate_weight[0], preferred_element_type=jnp.float32)

time: 230 us -> 165 us (0.72)
  blocking collectives: 50.3 us -> 0 us
  Pallas kernels: 141 us -> 157 us
  between operations: 13.5 us -> 0.04 us
  waiting for transfers between devices: 11.5 us -> 0 us
  local copies, waits for them, and re-layouts: 8.05 us -> 3.39 us
    all_gather x1 -> x0, blocking collectives: 46.6 us -> none  [small_rows(): return lax.all_gather(packed, 'expert', axis=0, tiled=True)]
    pallas_call x1, Pallas kernels: 141 us -> 157 us  [gathered_features(): pl.pallas_call(gather_kernel, out_shape=jax.ShapeDtypeStruct((SEQS, width...]
    unnamed x2 -> x0, waiting for transfers between devices: 11.5 us -> none
    unnamed x5 -> x3, local copies, waits for them, and re-layouts: 6.38 us -> 1.74 us
    psum x1 -> x0, blocking collectives: 3.69 us -> none  [small_rows(): lax.psum(jnp.dot(out_grad, proj_grad, preferred_element_type=jnp.float32)...]
  transfers between devices with their start and end apart: 1 -> 0, of which waited for: 1 -> 0; matrix products, arithmetic and copies ran while one was open for 0% -> 0% of each run, Pallas kernels for 0% -> 0%
where the time goes in v3:
time: 165 us
  Pallas kernels  157 us (95%)
  local copies, waits for them, and re-layouts  3.39 us (2%)
  other arithmetic  2.97 us (2%)
    pallas_call x1, Pallas kernels, gathered_features(): pl.pallas_call(gather_kernel, out_shape=jax.ShapeDtypeStruct((SEQS, width...  157 us

profile of v3, /device:TPU:0, one launch (start us, length us, event | category | flops | bytes accessed | tf_op | source)
XLA Modules:
  0.0 164.7 jit_solution(6977518937502996267)
XLA Ops:
  0.0 0.0 copy-start
  0.0 0.7 convert_bitcast_fusion
  0.7 0.8 select_reduce_fusion
  1.6 0.7 select_reduce_fusion.1
  2.3 0.1 copy.21
  2.4 0.0 copy-done
  2.4 1.4 fusion
  3.8 0.7 select_maximum_fusion.small_ref
  4.5 1.7 %copy.23.ph_ref = bf16[1024,64]{1,0:T(8,128)(2,1)} copy(bf16[1024,64]{0,1:T(8,128)(2,1)} %param.14) | data formatting | bytes 262144 | tf_op args[4]
  6.2 156.9 %shard_map.100 = f32[4,32,64]{2,1,0:T(8,128)} custom-call(bf16[128,3584]{1,0:T(8,128)(2,1)} %tok_ref.1, bf16[1,7168,1024]{2,1,0:T(8,128)(2,1)} %wg_ref.1, bf16[1,7168,1024]{2,1,0:T(8,128)(2,1)} %wu_ref.1, bf16[1024,64]{1,0:T(8,128)(2,1)} %copy.23.ph_ref, f32[128,128]{1,0:T(8,128)} %select_maximum_fusion.small_ref), custom_call_target="tpu_custom_call" | custom-call | flops 60129542144 | bytes 30277632 | tf_op jit(solution)/shard_map/pallas_call | solution.py:328
  163.2 1.5 reshape.6
  (2 shorter events, 0.0 us)
Async XLA Ops:
  0.0 2.4 %copy-start = (bf16[128,3584]{1,0:T(8,128)(2,1)S(1)}, bf16[128,3584]{1,0:T(8,128)(2,1)}, u32[]{:S(2)}) copy-start(bf16[128,3584]{1,0:T(8,128)(2,1)} %param.11) | copy-start | bytes 2752516
